TPU v7x, 512 devices: a whole 4x4x16 slice. The times are simulated.
512 devices in a mesh: row: 16 (over z), col: 32 (over y, x, core).
Axes of the slice: x: 4, y: 4, z: 16, core: 2. Of those that a mesh axis runs over, the one named last changes fastest.
Arguments:
- counts: int32 [16, 32], P('row', 'col'), may hold values from 1 to 16, as said below
- block_rows: int32 [16, 32, 16], P('row', 'col'), may hold values from 0 to 31, as said below
- block_cols: int32 [16, 32, 16], P('row', 'col'), may hold values from 0 to 15, as said below
- values: bfloat16 [16, 32, 16, 128, 128], P('row', 'col'), may hold values from -0.1875 to 0.1875
- start_block: float32 [64, 65536], P(None, ('row', 'col')), may hold values from -6 to 6
Outputs:
- diag_blocks: float32 [4, 64, 64], replicated
- off_blocks: float32 [4, 64, 64], replicated
- next_basis: float32 [64, 65536], P(None, ('row', 'col'))
Inputs may be any that keep to these rules, and one draw needn't show every extreme that they name: Each tile has 16 slots; only the first counts[r, c] are live. In every draw some tile has all 16 live. `block_rows`: block row within the tile's row tile; the global block row of a stored block never exceeds its global block column. `block_cols`: index r2 of the block column r2 * 32 + c of tile (r, c); r2 >= r.
All inputs are finite; a program needn't handle non-finite values.
Results may differ from a plain program's by a relative error of at most 0.04.
Values may be sent and summed in bfloat16 or wider, within the bound.
A program may use at most 64 MiB of HBM per device.

v0:
```python
import jax
import jax.numpy as jnp
from jax import lax
from jax.sharding import PartitionSpec as P

STEPS = 4


exact_mode = lax.Precision.HIGHEST


def full_dot(left, right):
    return jnp.dot(left, right, precision=exact_mode, preferred_element_type=jnp.float32)


def outer_gram(left, right):
    return lax.dot_general(
        left,
        right,
        (((1,), (1,)), ((), ())),
        precision=exact_mode,
        preferred_element_type=jnp.float32,
    )


def per_device(counts, block_rows, block_cols, values, start_block):
    row_devices = lax.axis_size("row")
    col_devices = lax.axis_size("col")
    live_count = counts[0, 0]
    row_slots = block_rows[0, 0]
    col_slots = block_cols[0, 0]
    tile_blocks = values[0, 0]
    slot_count = tile_blocks.shape[0]
    edge_size = tile_blocks.shape[1]
    block_width = start_block.shape[0]
    live_mask = (jnp.arange(slot_count, dtype=jnp.int32) < live_count).astype(jnp.float32)
    row_onehot = (row_slots[:, None] == jnp.arange(col_devices, dtype=jnp.int32)[None, :]).astype(
        jnp.float32
    ) * live_mask[:, None]
    col_onehot = (col_slots[:, None] == jnp.arange(row_devices, dtype=jnp.int32)[None, :]).astype(
        jnp.float32
    ) * live_mask[:, None]
    start_gram = lax.psum(outer_gram(start_block, start_block), ("row", "col"))
    factor = jnp.linalg.cholesky(start_gram)
    current = lax.linalg.triangular_solve(factor, start_block, left_side=True, lower=True)
    previous = None
    link_factor = factor
    diag_list = []
    link_list = []
    for turn_index in range(STEPS):
        own_rows = current
        own_narrow = own_rows.astype(jnp.bfloat16)
        col_inputs = lax.all_gather(own_narrow, "row", axis=1, tiled=True)
        row_inputs = lax.all_gather(own_narrow, "col", axis=1, tiled=True)
        row_grid = row_inputs.reshape(block_width, col_devices, edge_size)
        col_grid = col_inputs.reshape(block_width, row_devices, edge_size)
        picked_cols = jnp.take(col_grid, col_slots, axis=1)
        picked_rows = jnp.take(row_grid, row_slots, axis=1)
        upper_term = jnp.einsum(
            "dkj,kij->dki", picked_cols, tile_blocks, preferred_element_type=jnp.float32
        )
        lower_term = jnp.einsum(
            "dki,kij->dkj", picked_rows, tile_blocks, preferred_element_type=jnp.float32
        )
        row_part = jnp.einsum(
            "dki,kr->dri",
            upper_term,
            row_onehot,
            precision=exact_mode,
            preferred_element_type=jnp.float32,
        )
        col_part = jnp.einsum(
            "dkj,kc->dcj",
            lower_term,
            col_onehot,
            precision=exact_mode,
            preferred_element_type=jnp.float32,
        )
        row_part, col_part = (
            row_part.reshape(block_width, col_devices * edge_size),
            col_part.reshape(block_width, row_devices * edge_size),
        )
        col_share = lax.psum_scatter(
            col_part.astype(jnp.bfloat16), "row", scatter_dimension=1, tiled=True
        ).astype(jnp.float32)
        row_share = lax.psum_scatter(
            row_part.astype(jnp.bfloat16), "col", scatter_dimension=1, tiled=True
        ).astype(jnp.float32)
        image = current - (row_share + col_share)
        if previous is not None:
            image = image - full_dot(link_factor.T, previous)
        diag_block = lax.psum(outer_gram(image, own_rows), ("row", "col"))
        image = image - full_dot(diag_block, current)
        square_term = lax.psum(outer_gram(image, image), ("row", "col"))
        link_factor = jnp.linalg.cholesky(square_term)
        next_rows = lax.linalg.triangular_solve(link_factor, image, left_side=True, lower=True)
        diag_list.append(diag_block)
        link_list.append(link_factor)
        previous = current
        current = next_rows
    return (jnp.stack(diag_list), jnp.stack(link_list), current)


def solution(mesh):
    in_specs = (
        P("row", "col"),
        P("row", "col", None),
        P("row", "col", None),
        P("row", "col", None, None, None),
        P(None, ("row", "col")),
    )
    out_specs = (P(), P(), P(None, ("row", "col")))
    return jax.shard_map(
        per_device, mesh=mesh, in_specs=in_specs, out_specs=out_specs, check_vma=False
    )
```

profile of v0, /device:TPU:1, one launch (start us, length us, event | category | flops | bytes accessed | tf_op | source)
XLA Modules:
  0.0 1875.2 jit_solution(6830111939919045610)
XLA Ops:
  9.7 111.2 %psum.63 = f32[64,64]{0,1:T(8,128)S(1)} all-reduce(f32[64,64]{0,1:T(8,128)S(1)} %fusion.153), channel_id=1, replica_groups=mesh['row'=16,'col'=32] {'row','col'}, use_global_device_ids=true, to_apply=%region_0.0 | all-reduce | flops 4096 | bytes 32768 | tf_op jit(solution)/shard_map/psum | solution.py:43
  133.3 23.3 %all_gather.25 = bf16[64,4096]{1,0:T(8,128)(2,1)S(1)} all-gather(bf16[64,128]{1,0:T(8,128)(2,1)S(1)} %get-tuple-element.15), channel_id=1, replica_groups=mesh['row'=16,'col'=32] {'col'}, dimensions={1}, use_global_device_ids=true | all-gather | bytes 540672 | tf_op jit(solution)/shard_map/all_gather | solution.py:54
  160.3 21.5 %all_gather.24 = bf16[64,2048]{1,0:T(8,128)(2,1)S(1)} all-gather(bf16[64,128]{1,0:T(8,128)(2,1)S(1)} %get-tuple-element.15), channel_id=1, replica_groups=mesh['row'=16,'col'=32] {'row'}, dimensions={1}, use_global_device_ids=true | all-gather | bytes 278528 | tf_op jit(solution)/shard_map/all_gather | solution.py:53
  185.9 26.4 %reduce-scatter.27.cloned.1.call-done = bf16[128,64]{1,0:T(8,128)(2,1)} async-done(((bf16[2048,64]{1,0:T(8,128)(2,1)}), bf16[128,64]{1,0:T(8,128)(2,1)}) %reduce-scatter.27.cloned.1.call-update) | async-done | bytes 16400
  213.2 112.2 %reduce-scatter.25.cloned.1.call-done = bf16[128,64]{1,0:T(8,128)(2,1)} async-done(((bf16[4096,64]{1,0:T(8,128)(2,1)}), bf16[128,64]{1,0:T(8,128)(2,1)}) %reduce-scatter.25.cloned.1.call-update) | async-done | bytes 16400
  326.5 105.5 %psum.64 = f32[64,64]{1,0:T(8,128)S(1)} all-reduce(f32[64,64]{1,0:T(8,128)S(1)} %fusion.72), channel_id=1, replica_groups=mesh['row'=16,'col'=32] {'row','col'}, use_global_device_ids=true, to_apply=%region_5.0 | all-reduce | flops 4096 | bytes 32768 | tf_op jit(solution)/shard_map/psum | solution.py:92
  432.3 99.7 %psum.65 = f32[64,64]{0,1:T(8,128)S(1)} all-reduce(f32[64,64]{0,1:T(8,128)S(1)} %fusion.154), channel_id=1, replica_groups=mesh['row'=16,'col'=32] {'row','col'}, use_global_device_ids=true, to_apply=%region_6.0 | all-reduce | flops 4096 | bytes 32768 | tf_op jit(solution)/shard_map/psum | solution.py:94
  565.5 32.1 %all_gather.27 = bf16[64,4096]{1,0:T(8,128)(2,1)S(1)} all-gather(bf16[64,128]{1,0:T(8,128)(2,1)S(1)} %get-tuple-element.17), channel_id=1, replica_groups=mesh['row'=16,'col'=32] {'col'}, dimensions={1}, use_global_device_ids=true | all-gather | bytes 540672 | tf_op jit(solution)/shard_map/all_gather | solution.py:54
  604.8 47.9 %reduce-scatter.31.cloned.1.call-done = bf16[128,64]{1,0:T(8,128)(2,1)} async-done(((bf16[2048,64]{1,0:T(8,128)(2,1)}), bf16[128,64]{1,0:T(8,128)(2,1)}) %reduce-scatter.31.cloned.1.call-update) | async-done | bytes 16400
  653.5 111.8 %reduce-scatter.29.cloned.1.call-done = bf16[128,64]{1,0:T(8,128)(2,1)} async-done(((bf16[4096,64]{1,0:T(8,128)(2,1)}), bf16[128,64]{1,0:T(8,128)(2,1)}) %reduce-scatter.29.cloned.1.call-update) | async-done | bytes 16400
  767.2 105.5 %psum.66 = f32[64,64]{1,0:T(8,128)S(1)} all-reduce(f32[64,64]{1,0:T(8,128)S(1)} %fusion.155), channel_id=1, replica_groups=mesh['row'=16,'col'=32] {'row','col'}, use_global_device_ids=true, to_apply=%region_9.0 | all-reduce | flops 4096 | bytes 32768 | tf_op jit(solution)/shard_map/psum | solution.py:92
  873.0 99.8 %psum.67 = f32[64,64]{0,1:T(8,128)S(1)} all-reduce(f32[64,64]{0,1:T(8,128)S(1)} %fusion.156), channel_id=1, replica_groups=mesh['row'=16,'col'=32] {'row','col'}, use_global_device_ids=true, to_apply=%region_10.0 | all-reduce | flops 4096 | bytes 32768 | tf_op jit(solution)/shard_map/psum | solution.py:94
  985.3 21.6 %all_gather.28 = bf16[64,2048]{1,0:T(8,128)(2,1)S(1)} all-gather(bf16[64,128]{1,0:T(8,128)(2,1)S(1)} %get-tuple-element.19), channel_id=1, replica_groups=mesh['row'=16,'col'=32] {'row'}, dimensions={1}, use_global_device_ids=true | all-gather | bytes 278528 | tf_op jit(solution)/shard_map/all_gather | solution.py:53
  1006.9 31.0 %all_gather.29 = bf16[64,4096]{1,0:T(8,128)(2,1)S(1)} all-gather(bf16[64,128]{1,0:T(8,128)(2,1)S(1)} %get-tuple-element.19), channel_id=1, replica_groups=mesh['row'=16,'col'=32] {'col'}, dimensions={1}, use_global_device_ids=true | all-gather | bytes 540672 | tf_op jit(solution)/shard_map/all_gather | solution.py:54
  1045.2 47.5 %reduce-scatter.35.cloned.1.call-done = bf16[128,64]{1,0:T(8,128)(2,1)} async-done(((bf16[2048,64]{1,0:T(8,128)(2,1)}), bf16[128,64]{1,0:T(8,128)(2,1)}) %reduce-scatter.35.cloned.1.call-update) | async-done | bytes 16400
  1093.5 112.1 %reduce-scatter.33.cloned.1.call-done = bf16[128,64]{1,0:T(8,128)(2,1)} async-done(((bf16[4096,64]{1,0:T(8,128)(2,1)}), bf16[128,64]{1,0:T(8,128)(2,1)}) %reduce-scatter.33.cloned.1.call-update) | async-done | bytes 16400
  1207.5 105.5 %psum.68 = f32[64,64]{1,0:T(8,128)S(1)} all-reduce(f32[64,64]{1,0:T(8,128)S(1)} %fusion.157), channel_id=1, replica_groups=mesh['row'=16,'col'=32] {'row','col'}, use_global_device_ids=true, to_apply=%region_13.0 | all-reduce | flops 4096 | bytes 32768 | tf_op jit(solution)/shard_map/psum | solution.py:92
  1313.3 99.7 %psum.69 = f32[64,64]{0,1:T(8,128)S(1)} all-reduce(f32[64,64]{0,1:T(8,128)S(1)} %fusion.158), channel_id=1, replica_groups=mesh['row'=16,'col'=32] {'row','col'}, use_global_device_ids=true, to_apply=%region_14.0 | all-reduce | flops 4096 | bytes 32768 | tf_op jit(solution)/shard_map/psum | solution.py:94
  1425.5 21.4 %all_gather.30 = bf16[64,2048]{1,0:T(8,128)(2,1)S(1)} all-gather(bf16[64,128]{1,0:T(8,128)(2,1)S(1)} %get-tuple-element.21), channel_id=1, replica_groups=mesh['row'=16,'col'=32] {'row'}, dimensions={1}, use_global_device_ids=true | all-gather | bytes 278528 | tf_op jit(solution)/shard_map/all_gather | solution.py:53
  1446.9 31.2 %all_gather.31 = bf16[64,4096]{1,0:T(8,128)(2,1)S(1)} all-gather(bf16[64,128]{1,0:T(8,128)(2,1)S(1)} %get-tuple-element.21), channel_id=1, replica_groups=mesh['row'=16,'col'=32] {'col'}, dimensions={1}, use_global_device_ids=true | all-gather | bytes 540672 | tf_op jit(solution)/shard_map/all_gather | solution.py:54
  1485.3 48.0 %reduce-scatter.39.cloned.1.call-done = bf16[128,64]{1,0:T(8,128)(2,1)} async-done(((bf16[2048,64]{1,0:T(8,128)(2,1)}), bf16[128,64]{1,0:T(8,128)(2,1)}) %reduce-scatter.39.cloned.1.call-update) | async-done | bytes 16400
  1534.1 111.9 %reduce-scatter.37.cloned.1.call-done = bf16[128,64]{1,0:T(8,128)(2,1)} async-done(((bf16[4096,64]{1,0:T(8,128)(2,1)}), bf16[128,64]{1,0:T(8,128)(2,1)}) %reduce-scatter.37.cloned.1.call-update) | async-done | bytes 16400
  1647.9 105.5 %psum.70 = f32[64,64]{1,0:T(8,128)S(1)} all-reduce(f32[64,64]{1,0:T(8,128)S(1)} %fusion.159), channel_id=1, replica_groups=mesh['row'=16,'col'=32] {'row','col'}, use_global_device_ids=true, to_apply=%region_17.0 | all-reduce | flops 4096 | bytes 32768 | tf_op jit(solution)/shard_map/psum | solution.py:92
  1753.8 100.0 %psum.71 = f32[64,64]{0,1:T(8,128)S(1)} all-reduce(f32[64,64]{0,1:T(8,128)S(1)} %fusion.160), channel_id=1, replica_groups=mesh['row'=16,'col'=32] {'row','col'}, use_global_device_ids=true, to_apply=%region_18.0 | all-reduce | flops 4096 | bytes 32768 | tf_op jit(solution)/shard_map/psum | solution.py:94
  (138 shorter events, 127.5 us)
Async XLA Ops:
  7.2 150.1 %copy-start = (bf16[1,1,16,128,128]{4,3,2,1,0:T(8,128)(2,1)S(1)}, bf16[1,1,16,128,128]{4,3,2,1,0:T(8,128)(2,1)}, u32[]{:S(2)}) copy-start(bf16[1,1,16,128,128]{4,3,2,1,0:T(8,128)(2,1)} %param.15) | copy-start | bytes 1572868
  7.2 0.8 copy-start.2
  7.2 205.1 %reduce-scatter.27.cloned.1.call-start = ((), (), s32[]{:S(2)}) async-start(), calls=%async_computation.9 | async-start | bytes 557056
  127.4 5.6 copy-start.1
  157.6 0.7 copy-start.3
  160.2 165.2 %reduce-scatter.25.cloned.1.call-start = ((), (), s32[]{:S(2)}) async-start(), calls=%async_computation.8 | async-start | bytes 1081344
  185.9 466.8 %reduce-scatter.31.cloned.1.call-start = ((), (), s32[]{:S(2)}) async-start(), calls=%async_computation.11 | async-start | bytes 557056
  600.6 164.7 %reduce-scatter.29.cloned.1.call-start = ((), (), s32[]{:S(2)}) async-start(), calls=%async_computation.10 | async-start | bytes 1081344
  604.7 488.0 %reduce-scatter.35.cloned.1.call-start = ((), (), s32[]{:S(2)}) async-start(), calls=%async_computation.13 | async-start | bytes 557056
  1040.9 164.7 %reduce-scatter.33.cloned.1.call-start = ((), (), s32[]{:S(2)}) async-start(), calls=%async_computation.12 | async-start | bytes 1081344
  1045.2 488.1 %reduce-scatter.39.cloned.1.call-start = ((), (), s32[]{:S(2)}) async-start(), calls=%async_computation.15 | async-start | bytes 557056
  1481.2 164.8 %reduce-scatter.37.cloned.1.call-start = ((), (), s32[]{:S(2)}) async-start(), calls=%async_computation.14 | async-start | bytes 1081344
Sparse Core Ops, SparseCore 0:
  160.3 51.9 reduce-scatter.26
  217.3 108.0 reduce-scatter.24
  600.7 51.9 reduce-scatter.30
  657.5 107.7 reduce-scatter.28
  1041.0 51.6 reduce-scatter.34
  1097.5 108.0 reduce-scatter.32
  1481.3 51.9 reduce-scatter.38
  1538.2 107.6 reduce-scatter.36
where the time goes:
time: 1890 us; the launch traced here: 1880 us
  blocking collectives  1140 us (60%)
  waiting for transfers between devices  618 us (33%)
  other arithmetic  62.5 us (3%)
  local copies, waits for them, and re-layouts  24.2 us (1%)
  matrix products  19.2 us (1%)
    unnamed x16, waiting for transfers between devices  618 us
    psum x4, blocking collectives, per_device(): diag_block = lax.psum(outer_gram(image, own_rows), ('row', 'col'))  422 us
    psum x4, blocking collectives, per_device(): square_term = lax.psum(outer_gram(image, image), ('row', 'col'))  399 us
    all_gather x4, blocking collectives, per_device(): row_inputs = lax.all_gather(own_narrow, 'col', axis=1, tiled=True)  118 us
    psum x1, blocking collectives, per_device(): start_gram = lax.psum(outer_gram(start_block, start_block), ('row', 'col'))  111 us
    all_gather x4, blocking collectives, per_device(): col_inputs = lax.all_gather(own_narrow, 'row', axis=1, tiled=True)  85.5 us
  transfers between devices with their start and end apart: 8, of which 8 were waited for; matrix products, arithmetic and copies ran while one was open for 1% of the time, Pallas kernels for 0%

commit v1 on v0

v1 whole, which is shorter than its diff:
```python
import functools

import jax
import jax.numpy as jnp
from jax import lax
from jax.experimental import pallas as pl
from jax.experimental.pallas import tpu as pltpu
from jax.sharding import PartitionSpec as P

STEPS = 4
HI = lax.Precision.HIGHEST
F32 = jnp.float32
BF = jnp.bfloat16
MESH = pl.DeviceIdType.MESH


def mm(a, b):
    return lax.dot_general(
        a, b, (((1,), (0,)), ((), ())), precision=HI, preferred_element_type=F32
    )


def mm_nt(a, b):
    return lax.dot_general(
        a, b, (((1,), (1,)), ((), ())), precision=HI, preferred_element_type=F32
    )


def factor(gram):
    n = gram.shape[0]
    row = lax.broadcasted_iota(jnp.int32, (n, 2 * n), 0)
    lane = lax.broadcasted_iota(jnp.int32, (n, 2 * n), 1)
    eye = (row[:, :n] == lane[:, :n]).astype(F32)
    m = jnp.concatenate([gram, eye], axis=1)

    def body(k, m):
        pivot_row = jnp.sum(jnp.where(row == k, m, 0.0), axis=0, keepdims=True)
        at_k = lane == k
        col = jnp.sum(jnp.where(at_k, m, 0.0), axis=1, keepdims=True)
        pivot = jnp.sum(
            jnp.where(at_k[:1], pivot_row, 0.0), axis=1, keepdims=True
        )
        mult = jnp.where(row[:, :1] > k, col / pivot, 0.0)
        return m - mult * pivot_row

    m = lax.fori_loop(0, n, body, m)
    diag = jnp.sum(jnp.where(row == lane, m, 0.0), axis=1, keepdims=True)
    m = m / jnp.sqrt(diag)
    upper = jnp.where(lane[:, :n] >= row[:, :n], m[:, :n], 0.0)
    return upper, m[:, n:]


def kernel(
    nr,
    nc,
    tab,
    vals,
    start,
    diag_o,
    off_o,
    basis_o,
    vals_t,
    xcol,
    xrow,
    wcol,
    wrow,
    scol,
    srow,
    pcol,
    prow,
    rcol,
    rrow,
    ga,
    g1,
    g2,
    g3,
    q_s,
    qs_s,
    qp_s,
    v_s,
    e_s,
    ax_send,
    ax_recv,
    ay_send,
    ay_recv,
    bx_send,
    bx_recv,
    by_send,
    by_recv,
    g1_send,
    g1_recv,
    g2_send,
    g2_recv,
    g3_send,
    g3_recv,
):
    cap = vals.shape[0]
    width = start.shape[0]
    part = width // nc
    r = lax.axis_index("row")
    c = lax.axis_index("col")

    def on_col(i):
        return lax.rem(r + i, nr)

    def on_row(i):
        return lax.rem(c + i, nc)

    barrier = pltpu.get_barrier_semaphore()

    @pl.loop(1, nr)
    def _(i):
        pl.semaphore_signal(
            barrier, inc=1, device_id=(on_col(i), c), device_id_type=MESH
        )

    @pl.loop(1, nc)
    def _(i):
        pl.semaphore_signal(
            barrier, inc=1, device_id=(r, on_row(i)), device_id_type=MESH
        )

    def ag_col(par, to, slot):
        return pltpu.make_async_remote_copy(
            src_ref=xcol.at[par, r],
            dst_ref=xcol.at[par, slot],
            send_sem=ax_send.at[to],
            recv_sem=ax_recv.at[par, slot],
            device_id=(to, c),
            device_id_type=MESH,
        )

    def ag_row(par, to, slot):
        return pltpu.make_async_remote_copy(
            src_ref=xrow.at[par, c],
            dst_ref=xrow.at[par, slot],
            send_sem=ay_send.at[to],
            recv_sem=ay_recv.at[par, slot],
            device_id=(r, to),
            device_id_type=MESH,
        )

    def rs_col(par, to, slot):
        return pltpu.make_async_remote_copy(
            src_ref=pcol.at[to],
            dst_ref=rcol.at[par, slot],
            send_sem=bx_send.at[to],
            recv_sem=bx_recv.at[par, slot],
            device_id=(to, c),
            device_id_type=MESH,
        )

    def rs_row(par, to, slot):
        return pltpu.make_async_remote_copy(
            src_ref=prow.at[to],
            dst_ref=rrow.at[par, slot],
            send_sem=by_send.at[to],
            recv_sem=by_recv.at[par, slot],
            device_id=(r, to),
            device_id_type=MESH,
        )

    def gram_1(par, to, slot):
        return pltpu.make_async_remote_copy(
            src_ref=ga.at[to],
            dst_ref=g1.at[par, slot],
            send_sem=g1_send.at[to],
            recv_sem=g1_recv.at[par, slot],
            device_id=(r, to),
            device_id_type=MESH,
        )

    def gram_2(par, to, slot):
        return pltpu.make_async_remote_copy(
            src_ref=g2.at[par, r],
            dst_ref=g2.at[par, slot],
            send_sem=g2_send.at[to],
            recv_sem=g2_recv.at[par, slot],
            device_id=(to, c),
            device_id_type=MESH,
        )

    def gram_3(par, to, slot):
        return pltpu.make_async_remote_copy(
            src_ref=g3.at[par, c],
            dst_ref=g3.at[par, slot],
            send_sem=g3_send.at[to],
            recv_sem=g3_recv.at[par, slot],
            device_id=(r, to),
            device_id_type=MESH,
        )

    def send_all(copy, par, count, at, me):
        @pl.loop(1, count)
        def _(i):
            copy(par, at(i), me).start()

    def recv_all(copy, par, count, at):
        @pl.loop(1, count)
        def _(i):
            copy(par, at(i), at(i)).wait_recv()

    def sent_all(copy, par, count, at, me):
        @pl.loop(1, count)
        def _(i):
            copy(par, at(i), me).wait_send()

    def sum_begin(par, whole):
        for i in range(nc):
            ga[i] = whole[i * part : (i + 1) * part]
        g1[par, c] = ga[c]
        send_all(gram_1, par, nc, on_row, c)

    def sum_middle(par):
        recv_all(gram_1, par, nc, on_row)
        g2[par, r] = jnp.sum(g1[par], axis=0)
        send_all(gram_2, par, nr, on_col, r)
        sent_all(gram_1, par, nc, on_row, c)

    def sum_late(par):
        recv_all(gram_2, par, nr, on_col)
        g3[par, c] = jnp.sum(g2[par], axis=0)
        send_all(gram_3, par, nc, on_row, c)
        sent_all(gram_2, par, nr, on_col, r)

    def sum_end(par):
        recv_all(gram_3, par, nc, on_row)
        sent_all(gram_3, par, nc, on_row, c)
        return jnp.concatenate([g3[par, i] for i in range(nc)], axis=0)

    begin = start[...]
    gram = mm_nt(begin, begin)
    for k in range(cap):
        vals_t[k] = vals[k].T
    scol[cap] = jnp.zeros(scol.shape[1:], F32)
    srow[cap] = jnp.zeros(srow.shape[1:], F32)
    pl.semaphore_wait(barrier, nr + nc - 2)

    sum_begin(0, jnp.concatenate([gram, gram], axis=1))
    sum_middle(0)
    sum_late(0)
    total = sum_end(0)
    _, inverse = factor(total[:, :width])
    first = mm(inverse, begin)
    q_s[...] = first
    v_s[...] = first
    qp_s[...] = jnp.zeros_like(first)

    def coefficients(total, turn):
        a = total[:, :width]
        g = total[:, width:]
        upper, inverse = factor(g - mm_nt(a, a))
        row = lax.broadcasted_iota(jnp.int32, a.shape, 0)
        lane = lax.broadcasted_iota(jnp.int32, a.shape, 1)
        diag_o[turn] = a + (row == lane).astype(F32)
        off_o[turn] = upper.T
        return a, upper, inverse

    def step(turn, _):
        par = lax.rem(turn, 2)
        later = turn > 0
        narrow = v_s[...].astype(BF)
        xcol[par, r] = narrow
        xrow[par, c] = narrow

        @pl.when(later)
        def _():
            v = v_s[...]
            sum_begin(par, mm_nt(v, jnp.concatenate([q_s[...], v], axis=0)))

        send_all(ag_row, par, nc, on_row, c)
        send_all(ag_col, par, nr, on_col, r)

        @pl.when(later)
        def _():
            sum_middle(par)

        recv_all(ag_row, par, nc, on_row)
        wrow[...] = xrow[par]
        for k in range(cap):
            term = jnp.dot(
                wrow[tab[k]], vals[k], preferred_element_type=F32
            )
            scol[k] = term + scol[tab[2 * cap + k]]
        for i in range(nr):
            pcol[i] = scol[tab[4 * cap + nc + i]].astype(BF)
        rcol[par, r] = pcol[r]
        send_all(rs_col, par, nr, on_col, r)

        recv_all(ag_col, par, nr, on_col)
        wcol[...] = xcol[par]
        for k in range(cap):
            term = jnp.dot(
                wcol[tab[cap + k]], vals_t[k], preferred_element_type=F32
            )
            srow[k] = term + srow[tab[3 * cap + k]]
        for i in range(nc):
            prow[i] = srow[tab[4 * cap + i]].astype(BF)
        rrow[par, c] = prow[c]
        send_all(rs_row, par, nc, on_row, c)

        @pl.when(later)
        def _():
            sum_late(par)
            a, upper, inverse = coefficients(sum_end(par), turn - 1)
            q = q_s[...]
            base = jnp.concatenate(
                [v_s[...] - mm(a, q), mm(a, qs_s[...])], axis=1
            )
            base = mm(inverse, base)
            edge = q.shape[1]
            q_s[...] = base[:, :edge]
            qs_s[...] = base[:, edge:]
            qp_s[...] = mm(upper, q)
            e_s[...] = inverse

        recv_all(rs_row, par, nc, on_row)
        recv_all(rs_col, par, nr, on_col)
        share = jnp.sum(rrow[par].astype(F32), axis=0) + jnp.sum(
            rcol[par].astype(F32), axis=0
        )

        @pl.when(later)
        def _():
            image = mm(e_s[...], share) - qs_s[...]
            qs_s[...] = image
            v_s[...] = -image - qp_s[...]

        @pl.when(jnp.logical_not(later))
        def _():
            qs_s[...] = share
            v_s[...] = -share

        sent_all(ag_row, par, nc, on_row, c)
        sent_all(ag_col, par, nr, on_col, r)
        sent_all(rs_row, par, nc, on_row, c)
        sent_all(rs_col, par, nr, on_col, r)
        return 0

    lax.fori_loop(0, STEPS, step, 0)

    v = v_s[...]
    q = q_s[...]
    sum_begin(0, mm_nt(v, jnp.concatenate([q, v], axis=0)))
    sum_middle(0)
    sum_late(0)
    a, _, inverse = coefficients(sum_end(0), STEPS - 1)
    basis_o[...] = mm(inverse, v - mm(a, q))


def tables(counts, block_rows, block_cols, nr, nc):
    cap = block_rows.shape[0]
    slot = jnp.arange(cap, dtype=jnp.int32)
    every_row = jnp.arange(nc, dtype=jnp.int32)
    every_col = jnp.arange(nr, dtype=jnp.int32)
    live = jnp.broadcast_to(counts, (cap,))

    def latest(keys, wanted, below):
        hit = (keys[None, :] == wanted[:, None]) & (slot[None, :] < below[:, None])
        found = jnp.max(jnp.where(hit, slot[None, :], -1), axis=1)
        return jnp.where(found < 0, cap, found)

    return jnp.concatenate(
        [
            jnp.clip(block_rows, 0, nc - 1),
            jnp.clip(block_cols, 0, nr - 1),
            latest(block_cols, block_cols, slot),
            latest(block_rows, block_rows, slot),
            latest(block_rows, every_row, jnp.broadcast_to(counts, (nc,))),
            latest(block_cols, every_col, jnp.broadcast_to(counts, (nr,))),
        ]
    )


def per_device(counts, block_rows, block_cols, values, start_block):
    nr = lax.axis_size("row")
    nc = lax.axis_size("col")
    tab = tables(counts[0, 0], block_rows[0, 0], block_cols[0, 0], nr, nc)
    vals = values[0, 0]
    cap, edge, _ = vals.shape
    width = start_block.shape[0]
    part = width // nc
    vmem = pl.BlockSpec(memory_space=pltpu.VMEM)
    dma = pltpu.SemaphoreType.DMA

    def block(*lead, dtype=BF):
        return pltpu.VMEM((*lead, width, edge), dtype)

    def piece(*lead):
        return pltpu.VMEM((*lead, part, 2 * width), F32)

    return pl.pallas_call(
        functools.partial(kernel, nr, nc),
        out_shape=(
            jax.ShapeDtypeStruct((STEPS, width, width), F32),
            jax.ShapeDtypeStruct((STEPS, width, width), F32),
            jax.ShapeDtypeStruct((width, edge), F32),
        ),
        in_specs=[pl.BlockSpec(memory_space=pltpu.SMEM), vmem, vmem],
        out_specs=(vmem, vmem, vmem),
        scratch_shapes=[
            pltpu.VMEM((cap, edge, edge), BF),
            block(2, nr),
            block(2, nc),
            block(nr),
            block(nc),
            block(cap + 1, dtype=F32),
            block(cap + 1, dtype=F32),
            block(nr),
            block(nc),
            block(2, nr),
            block(2, nc),
            piece(nc),
            piece(2, nc),
            piece(2, nr),
            piece(2, nc),
            block(dtype=F32),
            block(dtype=F32),
            block(dtype=F32),
            block(dtype=F32),
            pltpu.VMEM((width, width), F32),
            dma((nr,)),
            dma((2, nr)),
            dma((nc,)),
            dma((2, nc)),
            dma((nr,)),
            dma((2, nr)),
            dma((nc,)),
            dma((2, nc)),
            dma((nc,)),
            dma((2, nc)),
            dma((nr,)),
            dma((2, nr)),
            dma((nc,)),
            dma((2, nc)),
        ],
        compiler_params=pltpu.CompilerParams(
            collective_id=0, has_side_effects=True, vmem_limit_bytes=40 << 20
        ),
        name="lanczos",
    )(tab, vals, start_block)


def solution(mesh):
    in_specs = (
        P("row", "col"),
        P("row", "col", None),
        P("row", "col", None),
        P("row", "col", None, None, None),
        P(None, ("row", "col")),
    )
    out_specs = (P(), P(), P(None, ("row", "col")))
    return jax.shard_map(
        per_device, mesh=mesh, in_specs=in_specs, out_specs=out_specs, check_vma=False
    )
```

time: 1890 us -> 224 us (0.12)
  blocking collectives: 1140 us -> 0 us
  waiting for transfers between devices: 618 us -> 0 us
  Pallas kernels: 0 us -> 216 us
  other arithmetic: 62.5 us -> 3.92 us
  local copies, waits for them, and re-layouts: 24.2 us -> 3.06 us
  matrix products: 19.2 us -> 0 us
    psum x9 -> x0, blocking collectives: 932 us -> none  [the longest x4 422 us: per_device(): diag_block = lax.psum(outer_gram(image, own_rows), ('row', 'col'))]
    unnamed x16 -> x0, waiting for transfers between devices: 618 us -> none
    pallas_call x0 -> x1, Pallas kernels: none -> 216 us  [per_device(): pl.pallas_call(functools.partial(kernel, nr, nc), out_shape=(jax.ShapeDty...]
    all_gather x8 -> x0, blocking collectives: 203 us -> none  [the longest x4 118 us: per_device(): row_inputs = lax.all_gather(own_narrow, 'col', axis=1, tiled=True)]
    another operation x27 -> x0, other arithmetic: 61.7 us -> none  [the longest x12 26.1 us: per_device(): link_factor = jnp.linalg.cholesky(square_term)]
  transfers between devices with their start and end apart: 8 -> 0, of which waited for: 8 -> 0; matrix products, arithmetic and copies ran while one was open for 1% -> 0% of each run, Pallas kernels for 0% -> 0%
where the time goes in v1:
time: 224 us
  Pallas kernels  216 us (96%)
  other arithmetic  3.92 us (2%)
  local copies, waits for them, and re-layouts  3.06 us (1%)
    pallas_call x1, Pallas kernels, per_device(): pl.pallas_call(functools.partial(kernel, nr, nc), out_shape=(jax.ShapeDty...  216 us

profile of v1, /device:TPU:1, one launch (start us, length us, event | category | flops | bytes accessed | tf_op | source)
XLA Modules:
  0.0 224.2 jit_solution(7656100580278488550)
XLA Ops:
  0.6 0.0 copy-start.1
  1.3 0.9 select_reduce_fusion.2
  2.2 0.7 select_reduce_fusion.1
  3.0 0.7 broadcast_clamp_fusion.1
  3.6 0.9 select_reduce_fusion
  4.6 0.7 compare_select_fusion.2
  5.2 0.1 concatenate.3.tab
  5.3 0.0 copy-done.1
  5.3 0.0 copy-start
  5.3 1.0 copy-done
  6.4 215.9 %lanczos.1 = (f32[4,64,64]{2,1,0:T(8,128)S(1)}, f32[4,64,64]{2,1,0:T(8,128)S(1)}, f32[64,128]{1,0:T(8,128)S(1)}) custom-call(s32[112]{0:T(128)S(1)} %concatenate.3.tab, bf16[16,128,128]{2,1,0:T(8,128)(2,1)S(1)} %bitcast.7, f32[64,128]{1,0:T(8,128)S(1)} %copy-done.1), custom_call_target="tpu_custom_call" | custom-call | tf_op jit(solution)/shard_map/lanczos/pallas_call | solution.py:392
  222.3 0.7 copy.12
  222.9 0.7 copy.13
  223.6 0.6 copy.14
  (3 shorter events, 0.0 us)
Async XLA Ops:
  0.6 4.7 %copy-start.1 = (f32[64,128]{1,0:T(8,128)S(1)}, f32[64,128]{1,0:T(8,128)}, u32[]{:S(2)}) copy-start(f32[64,128]{1,0:T(8,128)} %start.1) | copy-start | bytes 98308
  5.3 1.0 copy-start

commit v2 on v1

v2 whole, which is shorter than its diff:
```python
import functools

import jax
import jax.numpy as jnp
from jax import lax
from jax.experimental import pallas as pl
from jax.experimental.pallas import tpu as pltpu
from jax.sharding import PartitionSpec as P

STEPS = 4
HI = lax.Precision.HIGHEST
F32 = jnp.float32
BF = jnp.bfloat16
MESH = pl.DeviceIdType.MESH


def mm(a, b):
    return lax.dot_general(
        a, b, (((1,), (0,)), ((), ())), precision=HI, preferred_element_type=F32
    )


def mm_nt(a, b):
    return lax.dot_general(
        a, b, (((1,), (1,)), ((), ())), precision=HI, preferred_element_type=F32
    )


GROUP = 8


def factor(gram):
    n = gram.shape[0]
    row = lax.broadcasted_iota(jnp.int32, (n, 2 * n), 0)
    lane = lax.broadcasted_iota(jnp.int32, (n, 2 * n), 1)
    eye = (row[:, :n] == lane[:, :n]).astype(F32)
    m = jnp.concatenate([gram, eye], axis=1)
    above = lax.broadcasted_iota(jnp.int32, (GROUP, 2 * n), 0)
    done = []
    for first in range(0, n, GROUP):
        cols = [
            jnp.broadcast_to(m[:, first + j : first + j + 1], m.shape)
            for j in range(GROUP)
        ]
        for j in range(GROUP):
            inverse = 1.0 / cols[j][j : j + 1]
            head = jnp.where(above > j, cols[j][:GROUP], 0.0)
            mult = head if m.shape[0] == GROUP else jnp.concatenate(
                [head, cols[j][GROUP:]], axis=0
            )
            mult = mult * inverse
            for i in range(j + 1, GROUP):
                cols[i] = cols[i] - mult * cols[i][j : j + 1]
            m = m - mult * m[j : j + 1]
        done.append(m[:GROUP])
        m = m[GROUP:]
    m = jnp.concatenate(done, axis=0)
    diag = jnp.sum(jnp.where(row == lane, m, 0.0), axis=1, keepdims=True)
    m = m / jnp.sqrt(diag)
    upper = jnp.where(lane[:, :n] >= row[:, :n], m[:, :n], 0.0)
    return upper, m[:, n:]


def kernel(
    nr,
    nc,
    counts,
    block_rows,
    block_cols,
    vals_hbm,
    start_hbm,
    diag_o,
    off_o,
    basis_o,
    tab,
    vals,
    start,
    vals_t,
    xcol,
    xrow,
    wcol,
    wrow,
    scol,
    srow,
    pcol,
    psib,
    pown,
    pfin,
    rcol,
    rsib,
    rrow,
    ga,
    g1,
    g2,
    g3,
    q_s,
    qs_s,
    qp_s,
    v_s,
    e_s,
    load_sem,
    ax_send,
    ax_recv,
    ay_send,
    ay_recv,
    bx_send,
    bx_recv,
    bs_send,
    bs_recv,
    by_send,
    by_recv,
    g1_send,
    g1_recv,
    g2_send,
    g2_recv,
    g3_send,
    g3_recv,
):
    cap = vals.shape[0]
    width, edge = start.shape
    part = width // nc
    chips = nc // 2
    r = lax.axis_index("row")
    c = lax.axis_index("col")
    core = lax.rem(c, 2)
    chip = c // 2
    other = chip * 2 + 1 - core

    load_start = pltpu.make_async_copy(start_hbm, start, load_sem.at[0])
    load_vals = pltpu.make_async_copy(vals_hbm, vals, load_sem.at[1])
    load_start.start()
    load_vals.start()

    def on_col(i):
        return lax.rem(r + i, nr)

    def on_row(i):
        return lax.rem(c + i, nc)

    def on_chip(i):
        return lax.rem(chip + i, chips)

    xcol[...] = jnp.zeros_like(xcol)
    rcol[...] = jnp.zeros_like(rcol)

    barrier = pltpu.get_barrier_semaphore()

    @pl.loop(1, nr)
    def _(i):
        pl.semaphore_signal(
            barrier, inc=1, device_id=(on_col(i), c), device_id_type=MESH
        )

    @pl.loop(1, nc)
    def _(i):
        pl.semaphore_signal(
            barrier, inc=1, device_id=(r, on_row(i)), device_id_type=MESH
        )

    def remote(src, dst, send, recv, device):
        return pltpu.make_async_remote_copy(
            src_ref=src,
            dst_ref=dst,
            send_sem=send,
            recv_sem=recv,
            device_id=device,
            device_id_type=MESH,
        )

    def ag_col(par, to, slot):
        return remote(
            xcol.at[par, r],
            xcol.at[par, slot],
            ax_send.at[to],
            ax_recv.at[par, slot],
            (to, c),
        )

    def ag_row(par, to, slot):
        return remote(
            xrow.at[par, slot],
            xrow.at[par, slot],
            ay_send.at[to],
            ay_recv.at[par, slot],
            (r, to),
        )

    def ag_pass(par, at):
        return remote(
            xrow.at[par, at * 2 + core],
            xrow.at[par, at * 2 + core],
            ay_send.at[nc + at],
            ay_recv.at[par, at * 2 + core],
            (r, other),
        )

    def ag_passed(par, at):
        return remote(
            xrow.at[par, at * 2 + 1 - core],
            xrow.at[par, at * 2 + 1 - core],
            ay_send.at[nc + at],
            ay_recv.at[par, at * 2 + 1 - core],
            (r, other),
        )

    def rs_col(par, to, slot):
        return remote(
            pcol.at[to],
            rcol.at[par, slot],
            bx_send.at[to],
            bx_recv.at[par, slot],
            (to, c),
        )

    def rs_sib(par, i):
        return remote(
            psib.at[i],
            rsib.at[par, i],
            bs_send.at[i],
            bs_recv.at[par, i],
            (r, other),
        )

    def rs_row(par, i, to, slot):
        return remote(
            pfin.at[i],
            rrow.at[par, slot],
            by_send.at[i],
            by_recv.at[par, slot],
            (r, to * 2 + core),
        )

    def gram_1(par, to, slot):
        return remote(
            ga.at[to],
            g1.at[par, slot],
            g1_send.at[to],
            g1_recv.at[par, slot],
            (r, to),
        )

    def gram_2(par, to, slot):
        return remote(
            g2.at[par, r],
            g2.at[par, slot],
            g2_send.at[to],
            g2_recv.at[par, slot],
            (to, c),
        )

    def gram_3(par, to, slot):
        return remote(
            g3.at[par, c],
            g3.at[par, slot],
            g3_send.at[to],
            g3_recv.at[par, slot],
            (r, to),
        )

    def send_all(copy, par, count, at, me):
        @pl.loop(1, count)
        def _(i):
            copy(par, at(i), me).start()

    def recv_all(copy, par, count, at):
        @pl.loop(1, count)
        def _(i):
            copy(par, at(i), at(i)).wait_recv()

    def sent_all(copy, par, count, at, me):
        @pl.loop(1, count)
        def _(i):
            copy(par, at(i), me).wait_send()

    def sum_begin(par, whole):
        for i in range(nc):
            ga[i] = whole[i * part : (i + 1) * part]
        g1[par, c] = ga[c]
        send_all(gram_1, par, nc, on_row, c)

    def sum_middle(par):
        recv_all(gram_1, par, nc, on_row)
        g2[par, r] = jnp.sum(g1[par], axis=0)
        send_all(gram_2, par, nr, on_col, r)
        sent_all(gram_1, par, nc, on_row, c)

    def sum_late(par):
        recv_all(gram_2, par, nr, on_col)
        g3[par, c] = jnp.sum(g2[par], axis=0)
        send_all(gram_3, par, nc, on_row, c)
        sent_all(gram_2, par, nr, on_col, r)

    def sum_end(par):
        recv_all(gram_3, par, nc, on_row)
        sent_all(gram_3, par, nc, on_row, c)
        return jnp.concatenate([g3[par, i] for i in range(nc)], axis=0)

    at_prev_row, at_prev_col = 0, cap
    at_last_row = 2 * cap
    at_last_col = 2 * cap + nc
    live = counts[0]

    def latest(keys, want, below):
        found = jnp.int32(cap)
        for k in range(cap):
            hit = (keys[k] == want) & (k < below)
            found = jnp.where(hit, k, found)
        return found

    @pl.loop(0, cap)
    def _(k):
        tab[at_prev_row + k] = latest(block_rows, block_rows[k], k)
        tab[at_prev_col + k] = latest(block_cols, block_cols[k], k)

    @pl.loop(0, nc)
    def _(i):
        tab[at_last_row + i] = latest(block_rows, i, live)

    @pl.loop(0, nr)
    def _(i):
        tab[at_last_col + i] = latest(block_cols, i, live)

    load_start.wait()
    begin = start[...]
    gram = mm_nt(begin, begin)
    scol[cap] = jnp.zeros(scol.shape[1:], F32)
    srow[cap] = jnp.zeros(srow.shape[1:], F32)
    pl.semaphore_wait(barrier, nr + nc - 2)

    sum_begin(0, jnp.concatenate([gram, gram], axis=1))
    load_vals.wait()
    for k in range(cap):
        vals_t[k] = vals[k].T
    sum_middle(0)
    sum_late(0)
    total = sum_end(0)
    _, inverse = factor(total[:, :width])
    first = mm(inverse, begin)
    q_s[...] = first
    v_s[...] = first
    qp_s[...] = jnp.zeros_like(first)

    def coefficients(total, turn):
        a = total[:, :width]
        g = total[:, width:]
        upper, inverse = factor(g - mm_nt(a, a))
        row = lax.broadcasted_iota(jnp.int32, a.shape, 0)
        lane = lax.broadcasted_iota(jnp.int32, a.shape, 1)
        diag_o[turn] = a + (row == lane).astype(F32)
        off_o[turn] = upper.T
        return a, upper, inverse

    def step(turn, _):
        par = lax.rem(turn, 2)
        later = turn > 0
        narrow = v_s[...].astype(BF)
        xrow[par, c] = narrow
        xcol[par, r] = narrow

        @pl.loop(1, chips)
        def _(i):
            ag_row(par, on_chip(i) * 2 + core, c).start()

        ag_pass(par, chip).start()

        @pl.loop(0, r)
        def _(to):
            ag_col(par, to, r).start()

        @pl.when(later)
        def _():
            v = v_s[...]
            sum_begin(par, mm_nt(v, jnp.concatenate([q_s[...], v], axis=0)))

        @pl.loop(1, chips)
        def _(i):
            at = on_chip(i)
            ag_row(par, at * 2 + core, at * 2 + core).wait_recv()
            ag_pass(par, at).start()

        @pl.when(later)
        def _():
            sum_middle(par)

        @pl.loop(0, chips)
        def _(i):
            ag_passed(par, on_chip(i)).wait_recv()

        wrow[...] = xrow[par]
        for k in range(cap):
            term = jnp.dot(
                wrow[block_rows[k]], vals[k], preferred_element_type=F32
            )
            scol[k] = term + scol[tab[at_prev_col + k]]
        for i in range(nr):
            pcol[i] = scol[tab[at_last_col + i]].astype(BF)
        rcol[par, r] = pcol[r]

        @pl.loop(0, nr - 1 - r)
        def _(i):
            rs_col(par, nr - 1 - i, r).start()

        @pl.when(later)
        def _():
            sum_late(par)

        @pl.loop(r + 1, nr)
        def _(i):
            ag_col(par, i, i).wait_recv()

        wcol[...] = xcol[par]
        for k in range(cap):
            term = jnp.dot(
                wcol[block_cols[k]], vals_t[k], preferred_element_type=F32
            )
            srow[k] = term + srow[tab[at_prev_row + k]]
        for i in range(chips):
            at = at_last_row + on_chip(i + 1) * 2
            psib[i] = srow[tab[at + 1 - core]].astype(BF)
            pown[i] = srow[tab[at + core]]
            rs_sib(par, i).start()
        for i in range(chips):
            rs_sib(par, i).wait_recv()
            both = pown[i] + rsib[par, i].astype(F32)
            if i < chips - 1:
                pfin[i] = both.astype(BF)
                rs_row(par, i, on_chip(i + 1), chip).start()
            else:
                rrow[par, chip] = both.astype(BF)

        @pl.when(later)
        def _():
            a, upper, inverse = coefficients(sum_end(par), turn - 1)
            q = q_s[...]
            base = jnp.concatenate(
                [v_s[...] - mm(a, q), mm(a, qs_s[...])], axis=1
            )
            base = mm(inverse, base)
            q_s[...] = base[:, :edge]
            qs_s[...] = base[:, edge:]
            qp_s[...] = mm(upper, q)
            e_s[...] = inverse

        @pl.loop(0, chips - 1)
        def _(i):
            rs_row(par, i, on_chip(i + 1), on_chip(i + 1)).wait_recv()

        @pl.loop(0, r)
        def _(i):
            rs_col(par, i, i).wait_recv()

        share = jnp.sum(rrow[par].astype(F32), axis=0) + jnp.sum(
            rcol[par].astype(F32), axis=0
        )

        @pl.when(later)
        def _():
            image = mm(e_s[...], share) - qs_s[...]
            qs_s[...] = image
            v_s[...] = -image - qp_s[...]

        @pl.when(jnp.logical_not(later))
        def _():
            qs_s[...] = share
            v_s[...] = -share

        @pl.loop(1, chips)
        def _(i):
            ag_row(par, on_chip(i) * 2 + core, c).wait_send()

        @pl.loop(0, chips)
        def _(i):
            ag_pass(par, i).wait_send()
            rs_sib(par, i).wait_send()

        @pl.loop(0, chips - 1)
        def _(i):
            rs_row(par, i, on_chip(i + 1), chip).wait_send()

        @pl.loop(0, r)
        def _(to):
            ag_col(par, to, r).wait_send()

        @pl.loop(0, nr - 1 - r)
        def _(i):
            rs_col(par, nr - 1 - i, r).wait_send()

        return 0

    lax.fori_loop(0, STEPS, step, 0)

    v = v_s[...]
    q = q_s[...]
    sum_begin(0, mm_nt(v, jnp.concatenate([q, v], axis=0)))
    sum_middle(0)
    sum_late(0)
    a, _, inverse = coefficients(sum_end(0), STEPS - 1)
    basis_o[...] = mm(inverse, v - mm(a, q))


def per_device(counts, block_rows, block_cols, values, start_block):
    nr = lax.axis_size("row")
    nc = lax.axis_size("col")
    cap, edge, _ = values.shape[2:]
    width = start_block.shape[0]
    part = width // nc
    chips = nc // 2
    smem = pl.BlockSpec(memory_space=pltpu.SMEM)
    vmem = pl.BlockSpec(memory_space=pltpu.VMEM)
    anywhere = pl.BlockSpec(memory_space=pl.ANY)
    dma = pltpu.SemaphoreType.DMA

    def block(*lead, dtype=BF):
        return pltpu.VMEM((*lead, width, edge), dtype)

    def piece(*lead):
        return pltpu.VMEM((*lead, part, 2 * width), F32)

    return pl.pallas_call(
        functools.partial(kernel, nr, nc),
        out_shape=(
            jax.ShapeDtypeStruct((STEPS, width, width), F32),
            jax.ShapeDtypeStruct((STEPS, width, width), F32),
            jax.ShapeDtypeStruct((width, edge), F32),
        ),
        in_specs=[smem, smem, smem, anywhere, anywhere],
        out_specs=(vmem, vmem, vmem),
        scratch_shapes=[
            pltpu.SMEM((2 * cap + nc + nr,), jnp.int32),
            pltpu.VMEM((cap, edge, edge), BF),
            block(dtype=F32),
            pltpu.VMEM((cap, edge, edge), BF),
            block(2, nr),
            block(2, nc),
            block(nr),
            block(nc),
            block(cap + 1, dtype=F32),
            block(cap + 1, dtype=F32),
            block(nr),
            block(chips),
            block(chips, dtype=F32),
            block(chips),
            block(2, nr),
            block(2, chips),
            block(2, chips),
            piece(nc),
            piece(2, nc),
            piece(2, nr),
            piece(2, nc),
            block(dtype=F32),
            block(dtype=F32),
            block(dtype=F32),
            block(dtype=F32),
            pltpu.VMEM((width, width), F32),
            dma((2,)),
            dma((nr,)),
            dma((2, nr)),
            dma((nc + chips,)),
            dma((2, nc)),
            dma((nr,)),
            dma((2, nr)),
            dma((chips,)),
            dma((2, chips)),
            dma((chips,)),
            dma((2, chips)),
            dma((nc,)),
            dma((2, nc)),
            dma((nr,)),
            dma((2, nr)),
            dma((nc,)),
            dma((2, nc)),
        ],
        compiler_params=pltpu.CompilerParams(
            collective_id=0, has_side_effects=True, vmem_limit_bytes=40 << 20
        ),
        name="lanczos",
    )(counts[0], block_rows[0, 0], block_cols[0, 0], values[0, 0], start_block)


def solution(mesh):
    in_specs = (
        P("row", "col"),
        P("row", "col", None),
        P("row", "col", None),
        P("row", "col", None, None, None),
        P(None, ("row", "col")),
    )
    out_specs = (P(), P(), P(None, ("row", "col")))
    return jax.shard_map(
        per_device, mesh=mesh, in_specs=in_specs, out_specs=out_specs, check_vma=False
    )
```

time: 224 us -> 167 us (0.75)
  Pallas kernels: 216 us -> 161 us
  other arithmetic: 3.92 us -> 0 us
    pallas_call x1, Pallas kernels: 216 us -> 161 us  [per_device(): pl.pallas_call(functools.partial(kernel, nr, nc), out_shape=(jax.ShapeDty...]
    reduce_max x3 -> x0, other arithmetic: 2.58 us -> none  [latest(): found = jnp.max(jnp.where(hit, slot[None, :], -1), axis=1)]
where the time goes in v2:
time: 167 us
  Pallas kernels  161 us (96%)
  local copies, waits for them, and re-layouts  4.38 us (3%)
    pallas_call x1, Pallas kernels, per_device(): pl.pallas_call(functools.partial(kernel, nr, nc), out_shape=(jax.ShapeDty...  161 us
    unnamed x11, local copies, waits for them, and re-layouts  4.38 us

profile of v2, /device:TPU:1, one launch (start us, length us, event | category | flops | bytes accessed | tf_op | source)
XLA Modules:
  0.0 166.8 jit_solution(7950889346165907249)
XLA Ops:
  1.3 0.0 copy-start.2
  1.3 0.0 copy-start.3
  1.3 0.6 copy-done.2
  1.9 0.0 copy-done.3
  1.9 0.0 copy-start
  2.0 1.0 copy-done
  3.0 0.0 copy-start.1
  3.0 0.8 copy-done.1
  3.7 161.1 %lanczos.1 = (f32[4,64,64]{2,1,0:T(8,128)S(1)}, f32[4,64,64]{2,1,0:T(8,128)S(1)}, f32[64,128]{1,0:T(8,128)S(1)}) custom-call(s32[1]{0:T(128)} %bitcast.4.counts, s32[16]{0:T(128)S(1)} %bitcast.6, s32[16]{0:T(128)S(1)} %bitcast.7, bf16[16,128,128]{2,1,0:T(8,128)(2,1)S(1)} %bitcast.5, f32[64,128]{1,0:T(8,128)S(1)} %copy-done.1), custom_call_target="tpu_custom_call" | custom-call | tf_op jit(solution)/shard_map/lanczos/pallas_call | solution.py:519
  164.9 0.7 copy.12
  165.5 0.7 copy.13
  166.2 0.6 copy.14
Async XLA Ops:
  1.3 0.7 copy-start.2
  1.3 0.7 copy-start.3
  1.9 1.0 copy-start
  3.0 0.8 copy-start.1

commit v3 on v2

--- a/solution.py
+++ b/solution.py
@@ -64,14 +64,17 @@
 def kernel(
     nr,
     nc,
-    counts,
-    block_rows,
-    block_cols,
+    counts_hbm,
+    rows_hbm,
+    cols_hbm,
     vals_hbm,
     start_hbm,
     diag_o,
     off_o,
     basis_o,
+    counts,
+    rows,
+    cols,
     tab,
     vals,
     start,
@@ -127,8 +130,16 @@
     other = chip * 2 + 1 - core
 
     load_start = pltpu.make_async_copy(start_hbm, start, load_sem.at[0])
-    load_vals = pltpu.make_async_copy(vals_hbm, vals, load_sem.at[1])
+    load_vals = pltpu.make_async_copy(vals_hbm.at[0, 0], vals, load_sem.at[1])
+    load_scalars = [
+        pltpu.make_async_copy(src, dst, load_sem.at[2 + i])
+        for i, (src, dst) in enumerate(
+            ((counts_hbm, counts), (rows_hbm, rows), (cols_hbm, cols))
+        )
+    ]
     load_start.start()
+    for load in load_scalars:
+        load.start()
     load_vals.start()
 
     def on_col(i):
@@ -257,68 +268,92 @@
             (r, to),
         )
 
-    def send_all(copy, par, count, at, me):
-        @pl.loop(1, count)
-        def _(i):
-            copy(par, at(i), me).start()
-
-    def recv_all(copy, par, count, at):
-        @pl.loop(1, count)
-        def _(i):
-            copy(par, at(i), at(i)).wait_recv()
-
-    def sent_all(copy, par, count, at, me):
-        @pl.loop(1, count)
-        def _(i):
-            copy(par, at(i), me).wait_send()
+    nx = min(4, chips)
+    ny = chips // nx
+    y, x = chip // nx, lax.rem(chip, nx)
+
+    def ring(d, n):
+        return min(d, n - d)
+
+    plane = sorted(
+        (
+            (dy, dx, dc)
+            for dy in range(ny)
+            for dx in range(nx)
+            for dc in range(2)
+            if (dy, dx, dc) != (0, 0, 0)
+        ),
+        key=lambda o: -(10 * (ring(o[0], ny) + ring(o[1], nx)) + o[2]),
+    )
+    far_row = []
+    for dy, dx, dc in plane:
+        at = lax.rem(y + dy, ny) * nx + lax.rem(x + dx, nx)
+        far_row.append(at * 2 + (core if dc == 0 else 1 - core))
+    far_chip = [at for dy, dx, dc in plane if dc == 0 for at in (
+        lax.rem(y + dy, ny) * nx + lax.rem(x + dx, nx),)]
+    far_col = [on_col(d) for d in sorted(range(1, nr), key=lambda d: -ring(d, nr))]
+
+    def send_all(copy, par, peers, me):
+        for to in peers:
+            copy(par, to, me).start()
+
+    def recv_all(copy, par, peers):
+        for to in reversed(peers):
+            copy(par, to, to).wait_recv()
+
+    def sent_all(copy, par, peers, me):
+        for to in peers:
+            copy(par, to, me).wait_send()
 
     def sum_begin(par, whole):
         for i in range(nc):
             ga[i] = whole[i * part : (i + 1) * part]
         g1[par, c] = ga[c]
-        send_all(gram_1, par, nc, on_row, c)
+        send_all(gram_1, par, far_row, c)
 
     def sum_middle(par):
-        recv_all(gram_1, par, nc, on_row)
+        recv_all(gram_1, par, far_row)
         g2[par, r] = jnp.sum(g1[par], axis=0)
-        send_all(gram_2, par, nr, on_col, r)
-        sent_all(gram_1, par, nc, on_row, c)
+        send_all(gram_2, par, far_col, r)
+        sent_all(gram_1, par, far_row, c)
 
     def sum_late(par):
-        recv_all(gram_2, par, nr, on_col)
+        recv_all(gram_2, par, far_col)
         g3[par, c] = jnp.sum(g2[par], axis=0)
-        send_all(gram_3, par, nc, on_row, c)
-        sent_all(gram_2, par, nr, on_col, r)
+        send_all(gram_3, par, far_row, c)
+        sent_all(gram_2, par, far_col, r)
 
     def sum_end(par):
-        recv_all(gram_3, par, nc, on_row)
-        sent_all(gram_3, par, nc, on_row, c)
+        recv_all(gram_3, par, far_row)
+        sent_all(gram_3, par, far_row, c)
         return jnp.concatenate([g3[par, i] for i in range(nc)], axis=0)
 
     at_prev_row, at_prev_col = 0, cap
     at_last_row = 2 * cap
     at_last_col = 2 * cap + nc
-    live = counts[0]
+    for load in load_scalars:
+        load.wait()
+    live = counts[0, 0]
 
     def latest(keys, want, below):
         found = jnp.int32(cap)
         for k in range(cap):
-            hit = (keys[k] == want) & (k < below)
+            hit = (keys[0, 0, k] == want) & (k < below)
             found = jnp.where(hit, k, found)
         return found
 
     @pl.loop(0, cap)
     def _(k):
-        tab[at_prev_row + k] = latest(block_rows, block_rows[k], k)
-        tab[at_prev_col + k] = latest(block_cols, block_cols[k], k)
+        tab[at_prev_row + k] = latest(rows, rows[0, 0, k], k)
+        tab[at_prev_col + k] = latest(cols, cols[0, 0, k], k)
 
     @pl.loop(0, nc)
     def _(i):
-        tab[at_last_row + i] = latest(block_rows, i, live)
+        tab[at_last_row + i] = latest(rows, i, live)
 
     @pl.loop(0, nr)
     def _(i):
-        tab[at_last_col + i] = latest(block_cols, i, live)
+        tab[at_last_col + i] = latest(cols, i, live)
 
     load_start.wait()
     begin = start[...]
@@ -357,31 +392,28 @@
         xrow[par, c] = narrow
         xcol[par, r] = narrow
 
-        @pl.loop(1, chips)
-        def _(i):
-            ag_row(par, on_chip(i) * 2 + core, c).start()
-
-        ag_pass(par, chip).start()
-
-        @pl.loop(0, r)
-        def _(to):
-            ag_col(par, to, r).start()
-
         @pl.when(later)
         def _():
             v = v_s[...]
             sum_begin(par, mm_nt(v, jnp.concatenate([q_s[...], v], axis=0)))
 
-        @pl.loop(1, chips)
-        def _(i):
-            at = on_chip(i)
-            ag_row(par, at * 2 + core, at * 2 + core).wait_recv()
-            ag_pass(par, at).start()
+        for at in far_chip:
+            ag_row(par, at * 2 + core, c).start()
+
+        ag_pass(par, chip).start()
+
+        @pl.loop(0, r)
+        def _(to):
+            ag_col(par, to, r).start()
 
         @pl.when(later)
         def _():
             sum_middle(par)
 
+        for at in reversed(far_chip):
+            ag_row(par, at * 2 + core, at * 2 + core).wait_recv()
+            ag_pass(par, at).start()
+
         @pl.loop(0, chips)
         def _(i):
             ag_passed(par, on_chip(i)).wait_recv()
@@ -389,7 +421,7 @@
         wrow[...] = xrow[par]
         for k in range(cap):
             term = jnp.dot(
-                wrow[block_rows[k]], vals[k], preferred_element_type=F32
+                wrow[rows[0, 0, k]], vals[k], preferred_element_type=F32
             )
             scol[k] = term + scol[tab[at_prev_col + k]]
         for i in range(nr):
@@ -400,10 +432,6 @@
         def _(i):
             rs_col(par, nr - 1 - i, r).start()
 
-        @pl.when(later)
-        def _():
-            sum_late(par)
-
         @pl.loop(r + 1, nr)
         def _(i):
             ag_col(par, i, i).wait_recv()
@@ -411,7 +439,7 @@
         wcol[...] = xcol[par]
         for k in range(cap):
             term = jnp.dot(
-                wcol[block_cols[k]], vals_t[k], preferred_element_type=F32
+                wcol[cols[0, 0, k]], vals_t[k], preferred_element_type=F32
             )
             srow[k] = term + srow[tab[at_prev_row + k]]
         for i in range(chips):
@@ -419,6 +447,11 @@
             psib[i] = srow[tab[at + 1 - core]].astype(BF)
             pown[i] = srow[tab[at + core]]
             rs_sib(par, i).start()
+
+        @pl.when(later)
+        def _():
+            sum_late(par)
+
         for i in range(chips):
             rs_sib(par, i).wait_recv()
             both = pown[i] + rsib[par, i].astype(F32)
@@ -432,12 +465,8 @@
         def _():
             a, upper, inverse = coefficients(sum_end(par), turn - 1)
             q = q_s[...]
-            base = jnp.concatenate(
-                [v_s[...] - mm(a, q), mm(a, qs_s[...])], axis=1
-            )
-            base = mm(inverse, base)
-            q_s[...] = base[:, :edge]
-            qs_s[...] = base[:, edge:]
+            q_s[...] = v_s[...] - mm(a, q)
+            qs_s[...] = mm(a, qs_s[...])
             qp_s[...] = mm(upper, q)
             e_s[...] = inverse
 
@@ -455,9 +484,12 @@
 
         @pl.when(later)
         def _():
-            image = mm(e_s[...], share) - qs_s[...]
+            both = jnp.concatenate([share - qs_s[...], q_s[...]], axis=1)
+            both = mm(e_s[...], both)
+            image = both[:, :edge]
             qs_s[...] = image
             v_s[...] = -image - qp_s[...]
+            q_s[...] = both[:, edge:]
 
         @pl.when(jnp.logical_not(later))
         def _():
@@ -505,9 +537,8 @@
     width = start_block.shape[0]
     part = width // nc
     chips = nc // 2
-    smem = pl.BlockSpec(memory_space=pltpu.SMEM)
     vmem = pl.BlockSpec(memory_space=pltpu.VMEM)
-    anywhere = pl.BlockSpec(memory_space=pl.ANY)
+    hbm = pl.BlockSpec(memory_space=pltpu.HBM)
     dma = pltpu.SemaphoreType.DMA
 
     def block(*lead, dtype=BF):
@@ -523,9 +554,12 @@
             jax.ShapeDtypeStruct((STEPS, width, width), F32),
             jax.ShapeDtypeStruct((width, edge), F32),
         ),
-        in_specs=[smem, smem, smem, anywhere, anywhere],
+        in_specs=[hbm] * 5,
         out_specs=(vmem, vmem, vmem),
         scratch_shapes=[
+            pltpu.SMEM(counts.shape, jnp.int32),
+            pltpu.SMEM(block_rows.shape, jnp.int32),
+            pltpu.SMEM(block_cols.shape, jnp.int32),
             pltpu.SMEM((2 * cap + nc + nr,), jnp.int32),
             pltpu.VMEM((cap, edge, edge), BF),
             block(dtype=F32),
@@ -552,7 +586,7 @@
             block(dtype=F32),
             block(dtype=F32),
             pltpu.VMEM((width, width), F32),
-            dma((2,)),
+            dma((5,)),
             dma((nr,)),
             dma((2, nr)),
             dma((nc + chips,)),
@@ -571,10 +605,10 @@
             dma((2, nc)),
         ],
         compiler_params=pltpu.CompilerParams(
-            collective_id=0, has_side_effects=True, vmem_limit_bytes=40 << 20
+            collective_id=0, has_side_effects=True, vmem_limit_bytes=60 << 20
         ),
         name="lanczos",
-    )(counts[0], block_rows[0, 0], block_cols[0, 0], values[0, 0], start_block)
+    )(counts, block_rows, block_cols, values, start_block)
 
 
 def solution(mesh):

time: 167 us -> 161 us (0.964)
  Pallas kernels: 161 us -> 157 us
    pallas_call x1, Pallas kernels: 161 us -> 157 us  [per_device(): pl.pallas_call(functools.partial(kernel, nr, nc), out_shape=(jax.ShapeDty...]
    unnamed x11 -> x7, local copies, waits for them, and re-layouts: 4.38 us -> 2.98 us
where the time goes in v3:
time: 161 us
  Pallas kernels  157 us (98%)
  local copies, waits for them, and re-layouts  2.98 us (2%)
    pallas_call x1, Pallas kernels, per_device(): pl.pallas_call(functools.partial(kernel, nr, nc), out_shape=(jax.ShapeDty...  157 us

profile of v3, /device:TPU:1, one launch (start us, length us, event | category | flops | bytes accessed | tf_op | source)
XLA Modules:
  0.0 161.2 jit_solution(14196134324711440126)
XLA Ops:
  1.3 156.9 %lanczos.1 = (f32[4,64,64]{2,1,0:T(8,128)}, f32[4,64,64]{2,1,0:T(8,128)}, f32[64,128]{1,0:T(8,128)}) custom-call(s32[1,1]{1,0:T(1,128)S(6)} %copy.11.counts_hbm, s32[1,1,16]{2,1,0:T(1,128)} %rows_hbm.1, s32[1,1,16]{2,1,0:T(1,128)} %cols_hbm.1, bf16[1,1,16,128,128]{4,3,2,1,0:T(8,128)(2,1)} %vals_hbm.1, f32[64,128]{1,0:T(8,128)} %start_hbm.1), custom_call_target="tpu_custom_call" | custom-call | tf_op jit(solution)/shard_map/lanczos/pallas_call | solution.py:550
  158.2 0.0 copy-start
  158.2 1.6 copy.12
  159.8 0.0 copy-done
  159.8 0.0 copy-start.1
  159.8 0.7 copy.13
  160.5 0.1 copy-done.1
  160.6 0.6 copy.14
Async XLA Ops:
  158.2 1.6 %copy-start = (f32[4,64,64]{2,1,0:T(8,128)S(1)}, f32[4,64,64]{2,1,0:T(8,128)}, u32[]{:S(2)}) copy-start(f32[4,64,64]{2,1,0:T(8,128)} %get-tuple-element.7) | copy-start | bytes 196612
  159.8 0.8 copy-start.1

commit v4 on v3

--- a/solution.py
+++ b/solution.py
@@ -62,6 +62,7 @@
 
 
 def kernel(
+    eager,
     nr,
     nc,
     counts_hbm,
@@ -72,6 +73,7 @@
     diag_o,
     off_o,
     basis_o,
+    gain_o,
     counts,
     rows,
     cols,
@@ -101,6 +103,7 @@
     qp_s,
     v_s,
     e_s,
+    gain_s,
     load_sem,
     ax_send,
     ax_recv,
@@ -356,24 +359,16 @@
         tab[at_last_col + i] = latest(cols, i, live)
 
     load_start.wait()
-    begin = start[...]
-    gram = mm_nt(begin, begin)
+    v_s[...] = start[...]
+    q_s[...] = jnp.zeros_like(q_s)
+    qs_s[...] = jnp.zeros_like(qs_s)
+    gain_s[...] = jnp.zeros_like(gain_s)
     scol[cap] = jnp.zeros(scol.shape[1:], F32)
     srow[cap] = jnp.zeros(srow.shape[1:], F32)
-    pl.semaphore_wait(barrier, nr + nc - 2)
-
-    sum_begin(0, jnp.concatenate([gram, gram], axis=1))
     load_vals.wait()
     for k in range(cap):
         vals_t[k] = vals[k].T
-    sum_middle(0)
-    sum_late(0)
-    total = sum_end(0)
-    _, inverse = factor(total[:, :width])
-    first = mm(inverse, begin)
-    q_s[...] = first
-    v_s[...] = first
-    qp_s[...] = jnp.zeros_like(first)
+    pl.semaphore_wait(barrier, nr + nc - 2)
 
     def coefficients(total, turn):
         a = total[:, :width]
@@ -381,21 +376,34 @@
         upper, inverse = factor(g - mm_nt(a, a))
         row = lax.broadcasted_iota(jnp.int32, a.shape, 0)
         lane = lax.broadcasted_iota(jnp.int32, a.shape, 1)
-        diag_o[turn] = a + (row == lane).astype(F32)
-        off_o[turn] = upper.T
+        here = jnp.maximum(turn, 0)
+        diag_o[here] = a + (row == lane).astype(F32)
+        off_o[here] = upper.T
+        if not eager:
+            square = jnp.sum(jnp.where(row == lane, g, 0.0), axis=0, keepdims=True)
+            gain = inverse * inverse * (square / width)
+            gain = jnp.sum(jnp.sum(gain, axis=1, keepdims=True), axis=0, keepdims=True)
+            gain_s[...] = jnp.maximum(gain_s[...], gain)
         return a, upper, inverse
 
     def step(turn, _):
         par = lax.rem(turn, 2)
-        later = turn > 0
-        narrow = v_s[...].astype(BF)
+        v = v_s[...]
+        gram = mm_nt(v, jnp.concatenate([q_s[...], v], axis=0))
+        if eager:
+            sum_begin(par, gram)
+            sum_middle(par)
+            sum_late(par)
+            a, upper, inverse = coefficients(sum_end(par), turn - 1)
+            q = q_s[...]
+            v = mm(inverse, v - mm(a, q))
+            q_s[...] = v
+            qp_s[...] = mm(upper, q)
+        narrow = v.astype(BF)
         xrow[par, c] = narrow
         xcol[par, r] = narrow
-
-        @pl.when(later)
-        def _():
-            v = v_s[...]
-            sum_begin(par, mm_nt(v, jnp.concatenate([q_s[...], v], axis=0)))
+        if not eager:
+            sum_begin(par, gram)
 
         for at in far_chip:
             ag_row(par, at * 2 + core, c).start()
@@ -406,8 +414,7 @@
         def _(to):
             ag_col(par, to, r).start()
 
-        @pl.when(later)
-        def _():
+        if not eager:
             sum_middle(par)
 
         for at in reversed(far_chip):
@@ -448,8 +455,7 @@
             pown[i] = srow[tab[at + core]]
             rs_sib(par, i).start()
 
-        @pl.when(later)
-        def _():
+        if not eager:
             sum_late(par)
 
         for i in range(chips):
@@ -461,8 +467,7 @@
             else:
                 rrow[par, chip] = both.astype(BF)
 
-        @pl.when(later)
-        def _():
+        if not eager:
             a, upper, inverse = coefficients(sum_end(par), turn - 1)
             q = q_s[...]
             q_s[...] = v_s[...] - mm(a, q)
@@ -482,19 +487,15 @@
             rcol[par].astype(F32), axis=0
         )
 
-        @pl.when(later)
-        def _():
+        if eager:
+            v_s[...] = -share - qp_s[...]
+        else:
             both = jnp.concatenate([share - qs_s[...], q_s[...]], axis=1)
             both = mm(e_s[...], both)
             image = both[:, :edge]
             qs_s[...] = image
             v_s[...] = -image - qp_s[...]
             q_s[...] = both[:, edge:]
-
-        @pl.when(jnp.logical_not(later))
-        def _():
-            qs_s[...] = share
-            v_s[...] = -share
 
         @pl.loop(1, chips)
         def _(i):
@@ -528,9 +529,10 @@
     sum_late(0)
     a, _, inverse = coefficients(sum_end(0), STEPS - 1)
     basis_o[...] = mm(inverse, v - mm(a, q))
-
-
-def per_device(counts, block_rows, block_cols, values, start_block):
+    gain_o[0] = jnp.max(gain_s[...])
+
+
+def lanczos(eager, counts, block_rows, block_cols, values, start_block):
     nr = lax.axis_size("row")
     nc = lax.axis_size("col")
     cap, edge, _ = values.shape[2:]
@@ -548,14 +550,15 @@
         return pltpu.VMEM((*lead, part, 2 * width), F32)
 
     return pl.pallas_call(
-        functools.partial(kernel, nr, nc),
+        functools.partial(kernel, eager, nr, nc),
         out_shape=(
             jax.ShapeDtypeStruct((STEPS, width, width), F32),
             jax.ShapeDtypeStruct((STEPS, width, width), F32),
             jax.ShapeDtypeStruct((width, edge), F32),
+            jax.ShapeDtypeStruct((1,), F32),
         ),
         in_specs=[hbm] * 5,
-        out_specs=(vmem, vmem, vmem),
+        out_specs=(vmem, vmem, vmem, pl.BlockSpec(memory_space=pltpu.SMEM)),
         scratch_shapes=[
             pltpu.SMEM(counts.shape, jnp.int32),
             pltpu.SMEM(block_rows.shape, jnp.int32),
@@ -586,6 +589,7 @@
             block(dtype=F32),
             block(dtype=F32),
             pltpu.VMEM((width, width), F32),
+            pltpu.VMEM((8, 128), F32),
             dma((5,)),
             dma((nr,)),
             dma((2, nr)),
@@ -605,10 +609,20 @@
             dma((2, nc)),
         ],
         compiler_params=pltpu.CompilerParams(
-            collective_id=0, has_side_effects=True, vmem_limit_bytes=60 << 20
+            collective_id=int(eager), has_side_effects=True, vmem_limit_bytes=60 << 20
         ),
-        name="lanczos",
+        name="eager" if eager else "lanczos",
     )(counts, block_rows, block_cols, values, start_block)
+
+
+GAIN = 2.0
+
+
+def per_device(*args):
+    *outs, gain = lanczos(False, *args)
+    return lax.cond(
+        gain[0] <= GAIN, lambda: tuple(outs), lambda: tuple(lanczos(True, *args)[:3])
+    )
 
 
 def solution(mesh):

time: 161 us -> 147 us (0.913)
  Pallas kernels: 157 us -> 142 us
    pallas_call x1, Pallas kernels: 157 us -> 142 us  [lanczos(): pl.pallas_call(functools.partial(kernel, eager, nr, nc), out_shape=(jax.S...]
where the time goes in v4:
time: 147 us
  Pallas kernels  142 us (97%)
  local copies, waits for them, and re-layouts  2.57 us (2%)
  between operations  2.08 us (1%)
    pallas_call x1, Pallas kernels, lanczos(): pl.pallas_call(functools.partial(kernel, eager, nr, nc), out_shape=(jax.S...  142 us

profile of v4, /device:TPU:1, one launch (start us, length us, event | category | flops | bytes accessed | tf_op | source)
XLA Modules:
  0.0 146.9 jit_solution(1363196494956319815)
XLA Ops:
  0.6 0.0 copy-start
  1.3 0.0 copy-start.1
  1.4 142.2 %lanczos.1 = (f32[4,64,64]{2,1,0:T(8,128)S(1)}, f32[4,64,64]{2,1,0:T(8,128)S(1)}, f32[64,128]{1,0:T(8,128)S(1)}, f32[1]{0:T(128)}) custom-call(s32[1,1]{1,0:T(1,128)S(6)} %copy.17.counts_hbm, s32[1,1,16]{2,1,0:T(1,128)} %rows_hbm.1, s32[1,1,16]{2,1,0:T(1,128)} %cols_hbm.1, bf16[1,1,16,128,128]{4,3,2,1,0:T(8,128)(2,1)} %vals_hbm.1, f32[64,128]{1,0:T(8,128)} %start_hbm.1), custom_call_target="tpu_custom_call" | custom-call | tf_op jit(solution)/shard_map/lanczos/pallas_call | solution.py:552
  144.3 0.0 copy-start.2
  144.3 0.0 copy-start.3
  144.3 0.0 copy-done
  144.3 0.0 copy-done.1
  144.3 0.6 copy-done.2
  144.9 0.0 copy-done.3
  145.0 0.7 copy.18
  145.6 0.7 copy.19
  146.3 0.6 copy.20
  (1 shorter events, 0.0 us)
Async XLA Ops:
  0.6 143.7 %copy-start = (bf16[1,1,16,128,128]{4,3,2,1,0:T(8,128)(2,1)S(1)}, bf16[1,1,16,128,128]{4,3,2,1,0:T(8,128)(2,1)}, u32[]{:S(2)}) copy-start(bf16[1,1,16,128,128]{4,3,2,1,0:T(8,128)(2,1)} %vals_hbm.1) | copy-start | bytes 1572868
  1.3 143.0 %copy-start.1 = (f32[64,128]{1,0:T(8,128)S(1)}, f32[64,128]{1,0:T(8,128)}, u32[]{:S(2)}) copy-start(f32[64,128]{1,0:T(8,128)} %start_hbm.1) | copy-start | bytes 98308
  144.3 0.7 copy-start.2
  144.3 0.7 copy-start.3

commit v5 on v4

--- a/solution.py
+++ b/solution.py
@@ -294,7 +294,8 @@
         far_row.append(at * 2 + (core if dc == 0 else 1 - core))
     far_chip = [at for dy, dx, dc in plane if dc == 0 for at in (
         lax.rem(y + dy, ny) * nx + lax.rem(x + dx, nx),)]
-    far_col = [on_col(d) for d in sorted(range(1, nr), key=lambda d: -ring(d, nr))]
+    far = sorted(range(1, nr), key=lambda d: -ring(d, nr))
+    far_col = [on_col(d) for d in far]
 
     def send_all(copy, par, peers, me):
         for to in peers:
@@ -318,17 +319,14 @@
         recv_all(gram_1, par, far_row)
         g2[par, r] = jnp.sum(g1[par], axis=0)
         send_all(gram_2, par, far_col, r)
-        sent_all(gram_1, par, far_row, c)
 
     def sum_late(par):
         recv_all(gram_2, par, far_col)
         g3[par, c] = jnp.sum(g2[par], axis=0)
         send_all(gram_3, par, far_row, c)
-        sent_all(gram_2, par, far_col, r)
 
     def sum_end(par):
         recv_all(gram_3, par, far_row)
-        sent_all(gram_3, par, far_row, c)
         return jnp.concatenate([g3[par, i] for i in range(nc)], axis=0)
 
     at_prev_row, at_prev_col = 0, cap
@@ -386,11 +384,26 @@
             gain_s[...] = jnp.maximum(gain_s[...], gain)
         return a, upper, inverse
 
+    def sent_last(par):
+        if not eager:
+            sent_all(gram_3, par, far_row, c)
+
+        @pl.loop(0, chips)
+        def _(i):
+            rs_sib(par, i).wait_send()
+
+        for i in range(chips - 1):
+            rs_row(par, i, far_chip[i], chip).wait_send()
+
+        @pl.loop(0, nr - 1 - r)
+        def _(i):
+            rs_col(par, nr - 1 - i, r).wait_send()
+
     def step(turn, _):
         par = lax.rem(turn, 2)
         v = v_s[...]
-        gram = mm_nt(v, jnp.concatenate([q_s[...], v], axis=0))
         if eager:
+            gram = mm_nt(v, jnp.concatenate([q_s[...], v], axis=0))
             sum_begin(par, gram)
             sum_middle(par)
             sum_late(par)
@@ -399,20 +412,25 @@
             v = mm(inverse, v - mm(a, q))
             q_s[...] = v
             qp_s[...] = mm(upper, q)
+            sent_all(gram_1, par, far_row, c)
+            sent_all(gram_2, par, far_col, r)
+            sent_all(gram_3, par, far_row, c)
         narrow = v.astype(BF)
         xrow[par, c] = narrow
         xcol[par, r] = narrow
+        for d in far:
+
+            @pl.when(r >= d)
+            def _():
+                ag_col(par, r - d, r).start()
+
         if not eager:
-            sum_begin(par, gram)
+            sum_begin(par, mm_nt(v, jnp.concatenate([q_s[...], v], axis=0)))
 
         for at in far_chip:
             ag_row(par, at * 2 + core, c).start()
 
         ag_pass(par, chip).start()
-
-        @pl.loop(0, r)
-        def _(to):
-            ag_col(par, to, r).start()
 
         if not eager:
             sum_middle(par)
@@ -420,6 +438,10 @@
         for at in reversed(far_chip):
             ag_row(par, at * 2 + core, at * 2 + core).wait_recv()
             ag_pass(par, at).start()
+
+        @pl.when(turn > 0)
+        def _():
+            sent_last(1 - par)
 
         @pl.loop(0, chips)
         def _(i):
@@ -435,9 +457,21 @@
             pcol[i] = scol[tab[at_last_col + i]].astype(BF)
         rcol[par, r] = pcol[r]
 
-        @pl.loop(0, nr - 1 - r)
+        for d in far:
+
+            @pl.when(r + d < nr)
+            def _():
+                rs_col(par, r + d, r).start()
+
+        for at in far_chip:
+            ag_row(par, at * 2 + core, c).wait_send()
+
+        @pl.loop(0, chips)
         def _(i):
-            rs_col(par, nr - 1 - i, r).start()
+            ag_pass(par, i).wait_send()
+
+        if not eager:
+            sent_all(gram_1, par, far_row, c)
 
         @pl.loop(r + 1, nr)
         def _(i):
@@ -450,7 +484,7 @@
             )
             srow[k] = term + srow[tab[at_prev_row + k]]
         for i in range(chips):
-            at = at_last_row + on_chip(i + 1) * 2
+            at = at_last_row + ([*far_chip, chip])[i] * 2
             psib[i] = srow[tab[at + 1 - core]].astype(BF)
             pown[i] = srow[tab[at + core]]
             rs_sib(par, i).start()
@@ -463,11 +497,16 @@
             both = pown[i] + rsib[par, i].astype(F32)
             if i < chips - 1:
                 pfin[i] = both.astype(BF)
-                rs_row(par, i, on_chip(i + 1), chip).start()
+                rs_row(par, i, far_chip[i], chip).start()
             else:
                 rrow[par, chip] = both.astype(BF)
 
+        @pl.loop(0, r)
+        def _(to):
+            ag_col(par, to, r).wait_send()
+
         if not eager:
+            sent_all(gram_2, par, far_col, r)
             a, upper, inverse = coefficients(sum_end(par), turn - 1)
             q = q_s[...]
             q_s[...] = v_s[...] - mm(a, q)
@@ -475,9 +514,8 @@
             qp_s[...] = mm(upper, q)
             e_s[...] = inverse
 
-        @pl.loop(0, chips - 1)
-        def _(i):
-            rs_row(par, i, on_chip(i + 1), on_chip(i + 1)).wait_recv()
+        for i in reversed(range(chips - 1)):
+            rs_row(par, i, far_chip[i], far_chip[i]).wait_recv()
 
         @pl.loop(0, r)
         def _(i):
@@ -497,27 +535,6 @@
             v_s[...] = -image - qp_s[...]
             q_s[...] = both[:, edge:]
 
-        @pl.loop(1, chips)
-        def _(i):
-            ag_row(par, on_chip(i) * 2 + core, c).wait_send()
-
-        @pl.loop(0, chips)
-        def _(i):
-            ag_pass(par, i).wait_send()
-            rs_sib(par, i).wait_send()
-
-        @pl.loop(0, chips - 1)
-        def _(i):
-            rs_row(par, i, on_chip(i + 1), chip).wait_send()
-
-        @pl.loop(0, r)
-        def _(to):
-            ag_col(par, to, r).wait_send()
-
-        @pl.loop(0, nr - 1 - r)
-        def _(i):
-            rs_col(par, nr - 1 - i, r).wait_send()
-
         return 0
 
     lax.fori_loop(0, STEPS, step, 0)
@@ -525,11 +542,15 @@
     v = v_s[...]
     q = q_s[...]
     sum_begin(0, mm_nt(v, jnp.concatenate([q, v], axis=0)))
+    sent_last((STEPS - 1) % 2)
     sum_middle(0)
     sum_late(0)
     a, _, inverse = coefficients(sum_end(0), STEPS - 1)
     basis_o[...] = mm(inverse, v - mm(a, q))
     gain_o[0] = jnp.max(gain_s[...])
+    sent_all(gram_1, 0, far_row, c)
+    sent_all(gram_2, 0, far_col, r)
+    sent_all(gram_3, 0, far_row, c)
 
 
 def lanczos(eager, counts, block_rows, block_cols, values, start_block):

time: 147 us -> 141 us (0.959)
  Pallas kernels: 142 us -> 136 us
    pallas_call x1, Pallas kernels: 142 us -> 136 us  [lanczos(): pl.pallas_call(functools.partial(kernel, eager, nr, nc), out_shape=(jax.S...]
where the time goes in v5:
time: 141 us
  Pallas kernels  136 us (96%)
  local copies, waits for them, and re-layouts  2.57 us (2%)
  between operations  2.08 us (1%)
    pallas_call x1, Pallas kernels, lanczos(): pl.pallas_call(functools.partial(kernel, eager, nr, nc), out_shape=(jax.S...  136 us

profile of v5, /device:TPU:1, one launch (start us, length us, event | category | flops | bytes accessed | tf_op | source)
XLA Modules:
  0.0 140.8 jit_solution(1134133961765433605)
XLA Ops:
  0.6 0.0 copy-start
  1.3 0.0 copy-start.1
  1.4 136.1 %lanczos.1 = (f32[4,64,64]{2,1,0:T(8,128)S(1)}, f32[4,64,64]{2,1,0:T(8,128)S(1)}, f32[64,128]{1,0:T(8,128)S(1)}, f32[1]{0:T(128)}) custom-call(s32[1,1]{1,0:T(1,128)S(6)} %copy.17.counts_hbm, s32[1,1,16]{2,1,0:T(1,128)} %rows_hbm.1, s32[1,1,16]{2,1,0:T(1,128)} %cols_hbm.1, bf16[1,1,16,128,128]{4,3,2,1,0:T(8,128)(2,1)} %vals_hbm.1, f32[64,128]{1,0:T(8,128)} %start_hbm.1), custom_call_target="tpu_custom_call" | custom-call | tf_op jit(solution)/shard_map/lanczos/pallas_call | solution.py:573
  138.2 0.0 copy-start.2
  138.2 0.0 copy-start.3
  138.2 0.0 copy-done
  138.2 0.0 copy-done.1
  138.2 0.6 copy-done.2
  138.8 0.0 copy-done.3
  138.9 0.7 copy.18
  139.5 0.7 copy.19
  140.2 0.6 copy.20
  (1 shorter events, 0.0 us)
Async XLA Ops:
  0.6 137.6 %copy-start = (bf16[1,1,16,128,128]{4,3,2,1,0:T(8,128)(2,1)S(1)}, bf16[1,1,16,128,128]{4,3,2,1,0:T(8,128)(2,1)}, u32[]{:S(2)}) copy-start(bf16[1,1,16,128,128]{4,3,2,1,0:T(8,128)(2,1)} %vals_hbm.1) | copy-start | bytes 1572868
  1.3 136.9 %copy-start.1 = (f32[64,128]{1,0:T(8,128)S(1)}, f32[64,128]{1,0:T(8,128)}, u32[]{:S(2)}) copy-start(f32[64,128]{1,0:T(8,128)} %start_hbm.1) | copy-start | bytes 98308
  138.2 0.7 copy-start.2
  138.2 0.7 copy-start.3
